TPU v7x, 128 devices: a whole 4x4x4 slice. The times are simulated.
128 devices in a mesh: img: 32 (over y, x, core), ch: 4 (over z).
Axes of the slice: x: 4, y: 4, z: 4, core: 2. Of those that a mesh axis runs over, the one named last changes fastest.
Arguments:
- canvas: bfloat16 [1024, 32, 1536], P('img', None, 'ch'), may hold values from -6 to 6
- screen_size: int32 [32, 2], P('img'), may hold values from 8 to 32, as said below
- tile_counts: int32 [32], replicated, may hold values from 1 to 32, 512 in all
- tile_offsets: int32 [1024, 2], P('img'), may hold values from 0 to 28, as said below
- cotangent: bfloat16 [1024, 4, 4, 1536], P('img', None, None, 'ch'), may hold values from -6 to 6
- dw_kernel: bfloat16 [49, 1536], P(None, 'ch'), may hold values from -0.875 to 0.875
- dw_bias: float32 [1536], P('ch'), may hold values from -3 to 3
- ln_gain: float32 [1536], replicated, may hold values from 0.5 to 1.5
- ln_bias: float32 [1536], replicated, may hold values from -0.5 to 0.5
- w_in: bfloat16 [1536, 6144], P(None, 'ch'), may hold values from -0.15625 to 0.15625
- b_in: float32 [6144], P('ch'), may hold values from -1 to 1
- w_out: bfloat16 [6144, 1536], P('ch'), may hold values from -0.078125 to 0.078125
- layer_scale: float32 [1536], replicated, may hold values from 0.25 to 2
Outputs:
- grad_canvas: float32 [1024, 32, 1536], P('img', None, 'ch')
Inputs may be any that keep to these rules, and one draw needn't show every extreme that they name: `tile_counts`: the counts sum to 512 and the largest is exactly 32. `screen_size`: some screenshot is 32 by 32 cells. `tile_offsets`: every slot's interior lies inside its screenshot.
All inputs are finite; a program needn't handle non-finite values.
Results may differ from a plain program's by a relative error of at most 0.0031.
Values may be sent and summed in bfloat16 or wider, within the bound.
No kernel may reach another device: no remote copies, remote signals or barrier semaphores. Data moves between devices by JAX's collectives and lax.ppermute only.
A program may use at most 128 MiB of HBM per device.

v0:
```python
import jax
import jax.numpy as jnp
from jax import lax
from jax.sharding import PartitionSpec as P

TS = 4
slope_coef = 0.7978845608
cubic_coef = 0.044715
norm_eps = 1e-06


def gelu_slope(pre_act):
    inner_arg = slope_coef * (pre_act + cubic_coef * pre_act * pre_act * pre_act)
    tangent = jnp.tanh(inner_arg)
    return 0.5 * (1.0 + tangent) + 0.5 * pre_act * (1.0 - tangent * tangent) * slope_coef * (
        1.0 + 3.0 * cubic_coef * pre_act * pre_act
    )


def depthwise(patches, kernel, bias):
    result = jnp.zeros((patches.shape[0], TS, TS, patches.shape[3]), jnp.float32) + bias
    for offset_r in range(7):
        for offset_c in range(7):
            result = result + patches[
                :, offset_r : offset_r + TS, offset_c : offset_c + TS, :
            ].astype(jnp.float32) * kernel[offset_r * 7 + offset_c].astype(jnp.float32)
    return result


def depthwise_back(upstream, kernel):
    result = jnp.zeros((upstream.shape[0], TS + 6, TS + 6, upstream.shape[3]), jnp.float32)
    for offset_r in range(7):
        for offset_c in range(7):
            result = result.at[:, offset_r : offset_r + TS, offset_c : offset_c + TS, :].add(
                upstream * kernel[offset_r * 7 + offset_c].astype(jnp.float32)
            )
    return result


def shards(
    canvas,
    screen_size,
    tile_counts,
    tile_offsets,
    cotangent,
    dw_kernel,
    dw_bias,
    ln_gain,
    ln_bias,
    w_in,
    b_in,
    w_out,
    layer_scale,
):
    owners = lax.axis_size("img")
    my_owner = lax.axis_index("img")
    my_part = lax.axis_index("ch")
    side = canvas.shape[0]
    share = canvas.shape[2]
    most = tile_offsets.shape[0]
    width = ln_gain.shape[0]
    framed_side = TS + 6
    per_pair = -(-most // owners)
    buffer_len = owners * per_pair
    lines = jnp.arange(side, dtype=jnp.int32)
    inside = (lines[:, None] < screen_size[0, 0]) & (lines[None, :] < screen_size[0, 1])
    masked = jnp.where(inside[:, :, None], canvas, jnp.zeros_like(canvas))
    framed = jnp.pad(masked, ((3, 3), (3, 3), (0, 0)))
    patches = jax.vmap(
        lambda corner: lax.dynamic_slice(
            framed, (corner[0], corner[1], jnp.int32(0)), (framed_side, framed_side, share)
        )
    )(tile_offsets)
    slots = jnp.arange(most, dtype=jnp.int32)
    owner_ids = jnp.arange(owners, dtype=jnp.int32)
    my_count = jnp.sum(jnp.where(owner_ids == my_owner, tile_counts, 0))
    classes = min(most, owners)
    slot_class = slots % classes
    base = slot_class * owners // classes
    spread_off = jnp.where(
        slot_class == 1, 1, jnp.where(slot_class == classes - 1, owners - 1, base)
    )
    target = (my_owner + spread_off) % owners
    source = (my_owner - spread_off) % owners
    pick = source * per_pair + slots // classes
    position = target * per_pair + slots // classes
    send_cot = jnp.zeros((buffer_len, TS, TS, share), jnp.bfloat16).at[position].set(cotangent)
    send_tiles = (
        jnp.zeros((buffer_len, framed_side, framed_side, share), jnp.bfloat16)
        .at[position]
        .set(patches)
    )
    got_tiles, got_cot = (
        lax.all_to_all(send_tiles, "img", split_axis=0, concat_axis=0, tiled=True),
        lax.all_to_all(send_cot, "img", split_axis=0, concat_axis=0, tiled=True),
    )
    mixed = depthwise(got_tiles[pick], dw_kernel, dw_bias).astype(jnp.bfloat16)
    cot_mine = got_cot[pick]
    gathered, cot_full = (
        lax.all_gather(mixed, "ch", axis=3, tiled=True),
        lax.all_gather(cot_mine, "ch", axis=3, tiled=True),
    )
    values = gathered.astype(jnp.float32)
    center = jnp.mean(values, axis=3, keepdims=True)
    spread = jnp.mean(jnp.square(values - center), axis=3, keepdims=True)
    inv_std = lax.rsqrt(spread + norm_eps)
    normed = (values - center) * inv_std
    scaled = (normed * ln_gain + ln_bias).astype(jnp.bfloat16)
    row_count = most * TS * TS
    pre_act = (
        jnp.dot(scaled.reshape(row_count, width), w_in, preferred_element_type=jnp.float32) + b_in
    )
    out_grad = (
        (layer_scale * cot_full.astype(jnp.float32)).astype(jnp.bfloat16).reshape(row_count, width)
    )
    hidden_grad = lax.dot_general(
        out_grad, w_out, (((1,), (1,)), ((), ())), preferred_element_type=jnp.float32
    )
    act_grad = (hidden_grad * gelu_slope(pre_act)).astype(jnp.bfloat16)
    partial_norm = lax.dot_general(
        act_grad, w_in, (((1,), (1,)), ((), ())), preferred_element_type=jnp.float32
    )
    first_channel = my_part * share
    norm_grad = lax.psum(partial_norm, "ch").reshape(most, TS, TS, width)
    weighted = norm_grad * ln_gain
    upstream_full = inv_std * (
        weighted
        - jnp.mean(weighted, axis=3, keepdims=True)
        - normed * jnp.mean(weighted * normed, axis=3, keepdims=True)
    )
    upstream = lax.dynamic_slice_in_dim(upstream_full, first_channel, share, 3)
    listed_mask = (slots < my_count).astype(jnp.float32)
    tile_grad = depthwise_back(upstream, dw_kernel)
    tile_grad = tile_grad.at[:, 3 : 3 + TS, 3 : 3 + TS, :].add(cot_mine.astype(jnp.float32))
    send_back = (
        jnp.zeros((buffer_len, framed_side, framed_side, share), jnp.float32)
        .at[pick]
        .set(tile_grad)
    )
    returned = lax.all_to_all(send_back, "img", split_axis=0, concat_axis=0, tiled=True)
    own_grads = returned[position] * listed_mask[:, None, None, None]
    span = jnp.arange(framed_side, dtype=jnp.int32)
    row_index = tile_offsets[:, 0][:, None, None] + span[None, :, None]
    col_index = tile_offsets[:, 1][:, None, None] + span[None, None, :]
    total = (
        jnp.zeros((side + 6, side + 6, share), jnp.float32).at[row_index, col_index].add(own_grads)
    )
    cropped = total[3 : 3 + side, 3 : 3 + side, :]
    return jnp.where(inside[:, :, None], cropped, jnp.zeros_like(cropped))


def solution(mesh):
    return jax.shard_map(
        shards,
        mesh=mesh,
        in_specs=(
            P("img", None, "ch"),
            P("img", None),
            P(),
            P("img", None),
            P("img", None, None, "ch"),
            P(None, "ch"),
            P("ch"),
            P(),
            P(),
            P(None, "ch"),
            P("ch"),
            P("ch", None),
            P(),
        ),
        out_specs=P("img", None, "ch"),
        check_vma=False,
    )
```

profile of v0, /device:TPU:0, one launch (start us, length us, event | category | flops | bytes accessed | tf_op | source)
XLA Modules:
  0.0 1014.0 jit_solution(13687951348938377667)
XLA Ops:
  27.0 81.8 %while.51 = (s32[]{:T(128)}, bf16[38,38,384]{2,1,0:T(8,128)(2,1)S(1)}, s32[32,3]{0,1:T(4,128)S(1)}, bf16[32,10,10,384]{3,2,1,0:T(8,128)(2,1)}, s32[]{:T(128)}) while((s32[]{:T(128)}, bf16[38,38,384]{2,1,0:T(8,128)(2,1)S(1)}, s32[32,3]{0,1:T(4,128)S(1)}, bf16[32,10,10,384]{3,2,1,0:T(8,128)(2,1)}, s32[]{:T(128)}) %tuple.286), condition=%wide.while_cond.50, body=%wide.while_body.50.sunk | while | flops 2 | bytes 201321 | solution.py:70
  111.1 11.1 %scatter_fusion = bf16[32,10,10,384]{3,2,1,0:T(8,128)(2,1)} fusion(bf16[32,10,10,384]{3,2,1,0:T(8,128)(2,1)} %broadcast_in_dim.34, s32[32]{0:T(128)S(1)} %fusion.33, bf16[32,10,10,384]{3,2,1,0:T(8,128)(2,1)} %get-tuple-element.612), kind=kCustom, calls=%fused_computation.3 | custom fusion | bytes 7372928 | tf_op jit(solution)/shard_map/scatter | solution.py:91
  131.9 48.5 %all-to-all-done = bf16[32,10,10,384]{3,2,1,0:T(8,128)(2,1)} async-done(((bf16[32,10,10,384]{3,2,1,0:T(8,128)(2,1)}), bf16[32,10,10,384]{3,2,1,0:T(8,128)(2,1)}, u32[]{:S(2)}, u32[]{:S(2)}) %all-to-all-start) | async-done | bytes 2457632 | tf_op jit(solution)/shard_map/all_to_all | solution.py:94
  185.6 30.9 %add_convert_fusion.1 = bf16[32,4,4,384]{3,2,1,0:T(4,128)(2,1)} fusion(bf16[32,10,10,384]{3,2,1,0:T(8,128)(2,1)} %gather_fusion, f32[384]{0:T(512)S(1)} %get-tuple-element.660, f32[384]{0:T(512)S(1)} %get-tuple-element.661, f32[384]{0:T(512)S(1)} %get-tuple-element.614, f32[384]{0:T(512)S(1)} %get-tuple-element.615, f32[384]{0:T(512)S(1)} %get-tuple-element.616, ...), kind=kLoop, calls=%fused_computation.99 | loop fusion | flops 29097984 | bytes 19737600 | tf_op jit(solution)/shard_map/convert_element_type | solution.py:97
  219.4 25.5 %all-gather.4.cloned.1.call-done = bf16[32,4,4,1536]{3,2,1,0:T(4,128)(2,1)} async-done(((bf16[32,4,4,384]{3,2,1,0:T(4,128)(2,1)}), bf16[32,4,4,1536]{3,2,1,0:T(4,128)(2,1)}) %all-gather.4.cloned.1.call-update) | async-done | bytes 1572880 | tf_op jit(solution)/shard_map/all_gather | solution.py:100
  261.9 11.7 %fusion.26 = f32[512,1536]{1,0:T(8,128)} fusion(bf16[1536,1536]{1,0:T(8,128)(2,1)} %param.122, f32[512,1536]{1,0:T(8,128)} %convolution_add_fusion, bf16[512,1536]{1,0:T(8,128)(2,1)S(1)} %reshape.2695, bf16[1536,1536]{1,0:T(8,128)(2,1)} %param.124), kind=kOutput, calls=%fused_computation.101 | convolution fusion | flops 4846780416 | bytes 17301504 | tf_op jit(solution)/shard_map/dot_general | solution.py:120
  278.9 71.7 %all-reduce.4.cloned.1.call-done = f32[512,1536]{1,0:T(8,128)} async-done(((f32[512,1536]{1,0:T(8,128)}), f32[512,1536]{1,0:T(8,128)}) %all-reduce.4.cloned.1.call-update) | async-done | bytes 3145744 | tf_op jit(solution)/shard_map/psum | solution.py:124
  368.0 10.8 %scatter-add.175 = f32[32,10,10,384]{3,2,1,0:T(8,128)} dynamic-update-slice(f32[32,10,10,384]{3,2,1,0:T(8,128)} %scatter-add.174, f32[32,4,4,384]{3,2,1,0:T(4,128)S(1)} %fusion.11, s32[]{:T(128)} %constant.1568.clone.1, s32[]{:T(128)} %bitcast.6, s32[]{:T(128)} %bitcast.7, s32[]{:T(128)} %constant.1568.clone.1) | dynamic-update-slice | bytes 1572868 | tf_op jit(solution)/shard_map/scatter-add | solution.py:34
  382.9 10.7 %scatter-add.176 = f32[32,10,10,384]{3,2,1,0:T(8,128)} dynamic-update-slice(f32[32,10,10,384]{3,2,1,0:T(8,128)} %scatter-add.175, f32[32,4,4,384]{3,2,1,0:T(4,128)S(1)} %add_select_fusion.4, s32[]{:T(128)} %constant.1568.clone.1, s32[]{:T(128)} %bitcast.8, s32[]{:T(128)} %bitcast.9, s32[]{:T(128)} %constant.1568.clone.1) | dynamic-update-slice | bytes 1572868 | tf_op jit(solution)/shard_map/scatter-add | solution.py:34
  397.5 10.5 %scatter-add.179 = f32[32,10,10,384]{3,2,1,0:T(8,128)} dynamic-update-slice(f32[32,10,10,384]{3,2,1,0:T(8,128)} %scatter-add.176, f32[32,4,4,384]{3,2,1,0:T(4,128)S(1)} %add_select_fusion.3, s32[]{:T(128)} %constant.1568.clone.1, s32[]{:T(128)} %bitcast.10, s32[]{:T(128)} %bitcast.11, s32[]{:T(128)} %constant.1568.clone.1) | dynamic-update-slice | bytes 1572868 | tf_op jit(solution)/shard_map/scatter-add | solution.py:34
  412.0 10.7 %scatter-add.180 = f32[32,10,10,384]{3,2,1,0:T(8,128)} dynamic-update-slice(f32[32,10,10,384]{3,2,1,0:T(8,128)} %scatter-add.179, f32[32,4,4,384]{3,2,1,0:T(4,128)S(1)} %add_select_fusion.2, s32[]{:T(128)} %constant.1568.clone.1, s32[]{:T(128)} %bitcast.12, s32[]{:T(128)} %bitcast.13, s32[]{:T(128)} %constant.1568.clone.1) | dynamic-update-slice | bytes 1572868 | tf_op jit(solution)/shard_map/scatter-add | solution.py:34
  426.8 10.7 %scatter-add.181 = f32[32,10,10,384]{3,2,1,0:T(8,128)} dynamic-update-slice(f32[32,10,10,384]{3,2,1,0:T(8,128)} %scatter-add.180, f32[32,4,4,384]{3,2,1,0:T(4,128)S(1)} %add_select_fusion.1, s32[]{:T(128)} %constant.1568.clone.1, s32[]{:T(128)} %bitcast.14, s32[]{:T(128)} %bitcast.15, s32[]{:T(128)} %constant.1568.clone.1) | dynamic-update-slice | bytes 1572868 | tf_op jit(solution)/shard_map/scatter-add | solution.py:34
  441.6 10.6 %scatter-add.184 = f32[32,10,10,384]{3,2,1,0:T(8,128)} dynamic-update-slice(f32[32,10,10,384]{3,2,1,0:T(8,128)} %scatter-add.181, f32[32,4,4,384]{3,2,1,0:T(4,128)S(1)} %add_select_fusion, s32[]{:T(128)} %constant.1568.clone.1, s32[]{:T(128)} %bitcast.16, s32[]{:T(128)} %bitcast.17, s32[]{:T(128)} %constant.1568.clone.1) | dynamic-update-slice | bytes 1572868 | tf_op jit(solution)/shard_map/scatter-add | solution.py:34
  518.0 9.4 scatter-add.199
  579.4 9.8 scatter-add.210
  590.9 9.4 scatter-add.211
  601.9 9.4 scatter-add.214
  616.1 9.4 scatter-add.216
  627.7 9.4 scatter-add.219
  775.1 9.5 scatter-add.246
  823.0 9.4 scatter-add.306
  836.5 15.6 %scatter_fusion.2 = f32[32,10,10,384]{3,2,1,0:T(8,128)} fusion(f32[32,10,10,384]{3,2,1,0:T(8,128)} %broadcast.1148, s32[32]{0:T(128)S(1)} %fusion.32, f32[32,10,10,384]{3,2,1,0:T(8,128)} %scatter-add.306), kind=kCustom, calls=%fused_computation.5 | custom fusion | bytes 14745728 | tf_op jit(solution)/shard_map/scatter | solution.py:138
  861.6 96.7 %all-to-all-done.2 = f32[32,10,10,384]{3,2,1,0:T(8,128)} async-done(((f32[32,10,10,384]{3,2,1,0:T(8,128)}), f32[32,10,10,384]{3,2,1,0:T(8,128)}, u32[]{:S(2)}, u32[]{:S(2)}) %all-to-all-start.2) | async-done | bytes 4915232 | tf_op jit(solution)/shard_map/all_to_all | solution.py:140
  979.9 22.7 %scatter_custom_fusion.3 = f32[1444,384]{1,0:T(8,128)S(1)} fusion(s32[3200]{0:T(1024)S(1)} %reshape.2834, f32[3200,384]{1,0:T(8,128)} %reshape.2836, f32[]{:T(128)} %constant.1567.clone.1), kind=kCustom, calls=%fused_computation.37 | custom fusion | flops 1228800 | bytes 2218496
  (269 shorter events, 526.3 us)
Async XLA Ops:
  12.2 110.0 %all-to-all-start.1 = ((bf16[32,4,4,384]{3,2,1,0:T(4,128)(2,1)}), bf16[32,4,4,384]{3,2,1,0:T(4,128)(2,1)S(1)}, u32[]{:S(2)}, u32[]{:S(2)}) async-start(bf16[32,4,4,384]{3,2,1,0:T(4,128)(2,1)} %scatter_fusion.1), calls=%async_computation.1 | async-start | bytes 786432 | tf_op jit(solution)/shard_map/all_to_all | solution.py:95
  122.2 7.7 copy-start.3
  122.2 58.2 %all-to-all-start = ((bf16[32,10,10,384]{3,2,1,0:T(8,128)(2,1)}), bf16[32,10,10,384]{3,2,1,0:T(8,128)(2,1)}, u32[]{:S(2)}, u32[]{:S(2)}) async-start(bf16[32,10,10,384]{3,2,1,0:T(8,128)(2,1)} %scatter_fusion), calls=%async_computation | async-start | bytes 7864320 | tf_op jit(solution)/shard_map/all_to_all | solution.py:94
  129.8 55.7 %copy-start.8 = (f32[384]{0:T(512)S(1)}, f32[384]{0:T(512)}, u32[]{:S(2)}) copy-start(f32[384]{0:T(512)} %param.119) | copy-start | bytes 4612
  129.9 86.7 %all-gather.6.cloned.1.call-start = ((), (), s32[]{:S(2)}) async-start(), calls=%async_computation.5 | async-start | bytes 1966080 | tf_op jit(solution)/shard_map/all_gather | solution.py:101
  131.9 113.0 %all-gather.4.cloned.1.call-start = ((), (), s32[]{:S(2)}) async-start(), calls=%async_computation.3 | async-start | bytes 1966080 | tf_op jit(solution)/shard_map/all_gather | solution.py:100
  185.6 31.0 %copy-start.5 = (f32[1536]{0:T(1024)S(1)}, f32[1536]{0:T(1024)}, u32[]{:S(2)}) copy-start(f32[1536]{0:T(1024)} %param.125) | copy-start | bytes 18436
  216.5 33.2 %copy-start.4 = (f32[1536]{0:T(1024)S(1)}, f32[1536]{0:T(1024)}, u32[]{:S(2)}) copy-start(f32[1536]{0:T(1024)} %param.120) | copy-start | bytes 18436
  216.5 33.2 %copy-start.6 = (f32[1536]{0:T(1024)S(1)}, f32[1536]{0:T(1024)}, u32[]{:S(2)}) copy-start(f32[1536]{0:T(1024)} %param.121) | copy-start | bytes 18436
  216.5 134.1 %all-reduce.4.cloned.1.call-start = ((), (), s32[]{:S(2)}) async-start(), calls=%async_computation.4 | async-start | bytes 6291456 | tf_op jit(solution)/shard_map/psum | solution.py:124
  249.7 5.1 copy-start.10
  261.9 15.5 %copy-start.7 = (s32[4]{0:T(128)S(1)}, s32[4]{0:T(128)}, u32[]{:S(2)}) copy-start(s32[4]{0:T(128)} %constant.1590.clone.1) | copy-start | bytes 52
  273.6 81.9 %copy-start = (bf16[32,4,4,1536]{3,2,1,0:T(4,128)(2,1)S(1)}, bf16[32,4,4,1536]{3,2,1,0:T(4,128)(2,1)}, u32[]{:S(2)}) copy-start(bf16[32,4,4,1536]{3,2,1,0:T(4,128)(2,1)} %all-gather.4.cloned.1.call-done) | copy-start | bytes 4718596
  355.5 4.6 copy-start.1
  795.6 25.7 %copy-start.2 = (bf16[32,4,4,384]{3,2,1,0:T(4,128)(2,1)S(1)}, bf16[32,4,4,384]{3,2,1,0:T(4,128)(2,1)}, u32[]{:S(2)}) copy-start(bf16[32,4,4,384]{3,2,1,0:T(4,128)(2,1)} %gather_fusion.1) | copy-start | bytes 1179652
  852.0 7.7 copy-start.9
  852.0 8.3 copy-start.11
  852.0 106.3 %all-to-all-start.2 = ((f32[32,10,10,384]{3,2,1,0:T(8,128)}), f32[32,10,10,384]{3,2,1,0:T(8,128)}, u32[]{:S(2)}, u32[]{:S(2)}) async-start(f32[32,10,10,384]{3,2,1,0:T(8,128)} %scatter_fusion.2), calls=%async_computation.2 | async-start | bytes 15728640 | tf_op jit(solution)/shard_map/all_to_all | solution.py:140
Sparse Core Ops, SparseCore 0:
  132.3 32.7 all-gather.5
  216.6 28.2 all-gather.3
  273.7 76.8 all-reduce.3
where the time goes:
time: 1030 us; the launch traced here: 1010 us
  local copies, waits for them, and re-layouts  516 us (50%)
  waiting for transfers between devices  242 us (23%)
  other arithmetic  200 us (19%)
  starting transfers between devices  22.4 us (2%)
  matrix products  18.8 us (2%)
  between operations  13.8 us (1%)
    scatter-add x37, local copies, waits for them, and re-layouts, depthwise_back(): result.at[:, offset_r:offset_r + TS, offset_c:offset_c + TS, :]  349 us
    all_to_all x1, waiting for transfers between devices, shards(): lax.all_to_all(send_back, 'img', split_axis=0, concat_axis=0, tiled=True)  96.7 us
    gather x96, local copies, waits for them, and re-layouts  81.8 us
    psum x1, waiting for transfers between devices, shards(): norm_grad = lax.psum(partial_norm, 'ch').reshape(most, TS, TS, width)  71.7 us
    add x31, other arithmetic, depthwise_back(): result.at[:, offset_r:offset_r + TS, offset_c:offset_c + TS, :]  57.6 us
    all_to_all x1, waiting for transfers between devices, shards(): lax.all_to_all(send_tiles, 'img', split_axis=0, concat_axis=0, tiled=True)  48.5 us
    scatter-add x12, other arithmetic, depthwise_back(): result.at[:, offset_r:offset_r + TS, offset_c:offset_c + TS, :]  32.1 us
    convert_element_type x1, other arithmetic, shards(): mixed = depthwise(got_tiles[pick], dw_kernel, dw_bias).astype(jnp.bfloat16)  30.9 us
  transfers between devices with their start and end apart: 6, of which 4 were waited for; matrix products, arithmetic and copies ran while one was open for 15% of the time, Pallas kernels for 0%

commit v1 on v0

--- a/solution.py
+++ b/solution.py
@@ -7,6 +7,28 @@
 slope_coef = 0.7978845608
 cubic_coef = 0.044715
 norm_eps = 1e-06
+
+
+def joined_along(blocks, dim):
+    blocks = jnp.moveaxis(blocks, 0, dim)
+    lengths = blocks.shape
+    return blocks.reshape(*lengths[:dim], lengths[dim] * lengths[dim + 1], *lengths[dim + 2 :])
+
+
+def ring_gather(shard, axis, dim):
+    size = lax.axis_size(axis)
+    pairs = [(i, (i + 1) % size) for i in range(size)]
+    back = [(b, a) for a, b in pairs]
+    lower, upper = ([], [])
+    for turn in range(size - 1):
+        if turn % 2 == 0:
+            lower.append(lax.ppermute(lower[-1] if lower else shard, axis, pairs))
+        else:
+            upper.append(lax.ppermute(upper[-1] if upper else shard, axis, back))
+    tiles = jnp.stack([*lower[::-1], shard, *upper])
+    shift = lax.axis_index(axis) - len(lower)
+    tiles = tiles[(jnp.arange(size) - shift) % size]
+    return joined_along(tiles, dim)
 
 
 def gelu_slope(pre_act):
@@ -97,7 +119,7 @@
     mixed = depthwise(got_tiles[pick], dw_kernel, dw_bias).astype(jnp.bfloat16)
     cot_mine = got_cot[pick]
     gathered, cot_full = (
-        lax.all_gather(mixed, "ch", axis=3, tiled=True),
+        ring_gather(mixed, "ch", 3),
         lax.all_gather(cot_mine, "ch", axis=3, tiled=True),
     )
     values = gathered.astype(jnp.float32)

time: 1030 us -> 1030 us (level)
  waiting for transfers between devices: 242 us -> 214 us
  other arithmetic: 200 us -> 213 us
    all_gather x1 -> x0, waiting for transfers between devices: 25.5 us -> none  [shards(): lax.all_gather(mixed, 'ch', axis=3, tiled=True)]
    another operation x10 -> x12, other arithmetic: 21.7 us -> 36.4 us
    unnamed x4 -> x5, other arithmetic: 23.2 us -> 26.7 us
    gather x96 -> x97, local copies, waits for them, and re-layouts: 81.8 us -> 84 us
  transfers between devices with their start and end apart: 6 -> 8, of which waited for: 4 -> 4; matrix products, arithmetic and copies ran while one was open for 15% -> 17% of each run, Pallas kernels for 0% -> 0%
where the time goes in v1:
time: 1030 us; the launch traced here: 1010 us
  local copies, waits for them, and re-layouts  525 us (51%)
  waiting for transfers between devices  214 us (21%)
  other arithmetic  213 us (21%)
  starting transfers between devices  27.3 us (3%)
  matrix products  18.6 us (2%)
  between operations  14.8 us (1%)
    scatter-add x37, local copies, waits for them, and re-layouts, depthwise_back(): result.at[:, offset_r:offset_r + TS, offset_c:offset_c + TS, :]  348 us
    all_to_all x1, waiting for transfers between devices, shards(): lax.all_to_all(send_back, 'img', split_axis=0, concat_axis=0, tiled=True)  96.7 us
    gather x96, local copies, waits for them, and re-layouts  81.8 us
    psum x1, waiting for transfers between devices, shards(): norm_grad = lax.psum(partial_norm, 'ch').reshape(most, TS, TS, width)  65.2 us
    add x31, other arithmetic, depthwise_back(): result.at[:, offset_r:offset_r + TS, offset_c:offset_c + TS, :]  57.7 us
    all_to_all x1, waiting for transfers between devices, shards(): lax.all_to_all(send_tiles, 'img', split_axis=0, concat_axis=0, tiled=True)  46.5 us
    scatter-add x12, other arithmetic, depthwise_back(): result.at[:, offset_r:offset_r + TS, offset_c:offset_c + TS, :]  32.1 us
    convert_element_type x1, other arithmetic, shards(): mixed = depthwise(got_tiles[pick], dw_kernel, dw_bias).astype(jnp.bfloat16)  30.5 us
  transfers between devices with their start and end apart: 8, of which 4 were waited for; matrix products, arithmetic and copies ran while one was open for 17% of the time, Pallas kernels for 0%

profile of v1, /device:TPU:0, one launch (start us, length us, event | category | flops | bytes accessed | tf_op | source)
XLA Modules:
  0.0 1011.8 jit_solution(11688979724497160857)
XLA Ops:
  27.6 81.8 %while.51 = (s32[]{:T(128)}, bf16[38,38,384]{2,1,0:T(8,128)(2,1)S(1)}, s32[32,3]{0,1:T(4,128)S(1)}, bf16[32,10,10,384]{3,2,1,0:T(8,128)(2,1)}, s32[]{:T(128)}) while((s32[]{:T(128)}, bf16[38,38,384]{2,1,0:T(8,128)(2,1)S(1)}, s32[32,3]{0,1:T(4,128)S(1)}, bf16[32,10,10,384]{3,2,1,0:T(8,128)(2,1)}, s32[]{:T(128)}) %tuple.286), condition=%wide.while_cond.50, body=%wide.while_body.50.sunk | while | flops 2 | bytes 201321 | solution.py:92
  111.6 11.1 %scatter_fusion = bf16[32,10,10,384]{3,2,1,0:T(8,128)(2,1)} fusion(bf16[32,10,10,384]{3,2,1,0:T(8,128)(2,1)} %broadcast_in_dim.34, s32[32]{0:T(128)S(1)} %fusion.39, bf16[32,10,10,384]{3,2,1,0:T(8,128)(2,1)} %get-tuple-element.612), kind=kCustom, calls=%fused_computation.4 | custom fusion | bytes 7372928 | tf_op jit(solution)/shard_map/scatter | solution.py:113
  134.6 46.5 %all-to-all-done = bf16[32,10,10,384]{3,2,1,0:T(8,128)(2,1)} async-done(((bf16[32,10,10,384]{3,2,1,0:T(8,128)(2,1)}), bf16[32,10,10,384]{3,2,1,0:T(8,128)(2,1)}, u32[]{:S(2)}, u32[]{:S(2)}) %all-to-all-start) | async-done | bytes 2457632 | tf_op jit(solution)/shard_map/all_to_all | solution.py:116
  186.2 30.5 %add_convert_fusion.2 = bf16[32,4,4,384]{3,2,1,0:T(4,128)(2,1)S(1)} fusion(bf16[32,10,10,384]{3,2,1,0:T(8,128)(2,1)} %gather_fusion, f32[384]{0:T(512)S(1)} %get-tuple-element.662, f32[384]{0:T(512)S(1)} %get-tuple-element.663, f32[384]{0:T(512)S(1)} %get-tuple-element.616, f32[384]{0:T(512)S(1)} %get-tuple-element.617, f32[384]{0:T(512)S(1)} %get-tuple-element.618, ...), kind=kLoop, calls=%fused_computation.107 | loop fusion | flops 29097984 | bytes 19737600 | tf_op jit(solution)/shard_map/convert_element_type | solution.py:119
  221.7 12.2 %fusion.59 = bf16[1,32,4,4,384]{4,3,2,1,0:T(4,128)(2,1)S(1)} fusion(f32[384]{0:T(512)S(1)} %get-tuple-element.662, bf16[32,10,10,384]{3,2,1,0:T(8,128)(2,1)S(1)} %copy-done, f32[384]{0:T(512)S(1)} %get-tuple-element.663, f32[384]{0:T(512)S(1)} %get-tuple-element.616, f32[384]{0:T(512)S(1)} %get-tuple-element.617, f32[384]{0:T(512)S(1)} %get-tuple-element.618, ...), kind=kLoop, calls=%fused_computation.248 | loop fusion | flops 29097984 | bytes 19737600 | tf_op jit(solution)/shard_map/stack | solution.py:28
  267.1 11.8 %fusion.31 = f32[512,1536]{1,0:T(8,128)} fusion(bf16[1536,1536]{1,0:T(8,128)(2,1)} %param.122, f32[512,1536]{1,0:T(8,128)} %convolution_add_fusion, bf16[512,1536]{1,0:T(8,128)(2,1)S(1)} %copy-done.5, bf16[1536,1536]{1,0:T(8,128)(2,1)} %param.124), kind=kOutput, calls=%fused_computation.109 | convolution fusion | flops 4846780416 | bytes 17301504 | tf_op jit(solution)/shard_map/dot_general | solution.py:142
  286.9 65.2 %all-reduce.4.cloned.1.call-done = f32[512,1536]{1,0:T(8,128)} async-done(((f32[512,1536]{1,0:T(8,128)}), f32[512,1536]{1,0:T(8,128)}) %all-reduce.4.cloned.1.call-update) | async-done | bytes 3145744 | tf_op jit(solution)/shard_map/psum | solution.py:146
  365.9 10.7 %scatter-add.175 = f32[32,10,10,384]{3,2,1,0:T(8,128)} dynamic-update-slice(f32[32,10,10,384]{3,2,1,0:T(8,128)} %scatter-add.174, f32[32,4,4,384]{3,2,1,0:T(4,128)S(1)} %fusion.13, s32[]{:T(128)} %constant.1584.clone.1, s32[]{:T(128)} %bitcast.12, s32[]{:T(128)} %bitcast.13, s32[]{:T(128)} %constant.1584.clone.1) | dynamic-update-slice | bytes 1572868 | tf_op jit(solution)/shard_map/scatter-add | solution.py:56
  380.6 10.5 %scatter-add.176 = f32[32,10,10,384]{3,2,1,0:T(8,128)} dynamic-update-slice(f32[32,10,10,384]{3,2,1,0:T(8,128)} %scatter-add.175, f32[32,4,4,384]{3,2,1,0:T(4,128)S(1)} %add_select_fusion.4, s32[]{:T(128)} %constant.1584.clone.1, s32[]{:T(128)} %bitcast.14, s32[]{:T(128)} %bitcast.15, s32[]{:T(128)} %constant.1584.clone.1) | dynamic-update-slice | bytes 1572868 | tf_op jit(solution)/shard_map/scatter-add | solution.py:56
  395.1 10.6 %scatter-add.179 = f32[32,10,10,384]{3,2,1,0:T(8,128)} dynamic-update-slice(f32[32,10,10,384]{3,2,1,0:T(8,128)} %scatter-add.176, f32[32,4,4,384]{3,2,1,0:T(4,128)S(1)} %add_select_fusion.3, s32[]{:T(128)} %constant.1584.clone.1, s32[]{:T(128)} %bitcast.16, s32[]{:T(128)} %bitcast.17, s32[]{:T(128)} %constant.1584.clone.1) | dynamic-update-slice | bytes 1572868 | tf_op jit(solution)/shard_map/scatter-add | solution.py:56
  409.7 10.5 %scatter-add.180 = f32[32,10,10,384]{3,2,1,0:T(8,128)} dynamic-update-slice(f32[32,10,10,384]{3,2,1,0:T(8,128)} %scatter-add.179, f32[32,4,4,384]{3,2,1,0:T(4,128)S(1)} %add_select_fusion.2, s32[]{:T(128)} %constant.1584.clone.1, s32[]{:T(128)} %bitcast.18, s32[]{:T(128)} %bitcast.19, s32[]{:T(128)} %constant.1584.clone.1) | dynamic-update-slice | bytes 1572868 | tf_op jit(solution)/shard_map/scatter-add | solution.py:56
  424.3 10.6 %scatter-add.181 = f32[32,10,10,384]{3,2,1,0:T(8,128)} dynamic-update-slice(f32[32,10,10,384]{3,2,1,0:T(8,128)} %scatter-add.180, f32[32,4,4,384]{3,2,1,0:T(4,128)S(1)} %add_select_fusion.1, s32[]{:T(128)} %constant.1584.clone.1, s32[]{:T(128)} %bitcast.20, s32[]{:T(128)} %bitcast.21, s32[]{:T(128)} %constant.1584.clone.1) | dynamic-update-slice | bytes 1572868 | tf_op jit(solution)/shard_map/scatter-add | solution.py:56
  438.9 10.5 %scatter-add.184 = f32[32,10,10,384]{3,2,1,0:T(8,128)} dynamic-update-slice(f32[32,10,10,384]{3,2,1,0:T(8,128)} %scatter-add.181, f32[32,4,4,384]{3,2,1,0:T(4,128)S(1)} %add_select_fusion, s32[]{:T(128)} %constant.1584.clone.1, s32[]{:T(128)} %bitcast.22, s32[]{:T(128)} %bitcast.23, s32[]{:T(128)} %constant.1584.clone.1) | dynamic-update-slice | bytes 1572868 | tf_op jit(solution)/shard_map/scatter-add | solution.py:56
  515.2 9.4 scatter-add.199
  576.8 9.4 scatter-add.210
  587.8 9.4 scatter-add.211
  598.9 9.4 scatter-add.214
  613.1 9.4 scatter-add.216
  624.6 9.4 scatter-add.219
  699.8 9.7 scatter-add.234
  820.4 9.4 scatter-add.306
  833.8 15.6 %scatter_fusion.2 = f32[32,10,10,384]{3,2,1,0:T(8,128)} fusion(f32[32,10,10,384]{3,2,1,0:T(8,128)} %broadcast.1228, s32[32]{0:T(128)S(1)} %copy-done.93, f32[32,10,10,384]{3,2,1,0:T(8,128)} %scatter-add.306), kind=kCustom, calls=%fused_computation.6 | custom fusion | bytes 14745728 | tf_op jit(solution)/shard_map/scatter | solution.py:160
  859.2 96.7 %all-to-all-done.2 = f32[32,10,10,384]{3,2,1,0:T(8,128)} async-done(((f32[32,10,10,384]{3,2,1,0:T(8,128)}), f32[32,10,10,384]{3,2,1,0:T(8,128)}, u32[]{:S(2)}, u32[]{:S(2)}) %all-to-all-start.2) | async-done | bytes 4915232 | tf_op jit(solution)/shard_map/all_to_all | solution.py:162
  977.5 22.7 %scatter_custom_fusion.3 = f32[1444,384]{1,0:T(8,128)S(1)} fusion(s32[3200]{0:T(1024)S(1)} %reshape.2920, f32[3200,384]{1,0:T(8,128)} %reshape.2922, f32[]{:T(128)} %constant.1583.clone.1), kind=kCustom, calls=%fused_computation.42 | custom fusion | flops 1228800 | bytes 2218496
  (460 shorter events, 546.0 us)
Async XLA Ops:
  6.6 105.1 %copy-start.90 = (s32[32]{0:T(128)}, s32[32]{0:T(128)S(1)}, u32[]{:S(2)}) copy-start(s32[32]{0:T(128)S(1)} %fusion.39) | copy-start | bytes 388
  12.2 110.6 %all-to-all-start.1 = ((bf16[32,4,4,384]{3,2,1,0:T(4,128)(2,1)}), bf16[32,4,4,384]{3,2,1,0:T(4,128)(2,1)S(1)}, u32[]{:S(2)}, u32[]{:S(2)}) async-start(bf16[32,4,4,384]{3,2,1,0:T(4,128)(2,1)} %scatter_fusion.1), calls=%async_computation.1 | async-start | bytes 786432 | tf_op jit(solution)/shard_map/all_to_all | solution.py:117
  122.8 58.2 %all-to-all-start = ((bf16[32,10,10,384]{3,2,1,0:T(8,128)(2,1)}), bf16[32,10,10,384]{3,2,1,0:T(8,128)(2,1)}, u32[]{:S(2)}, u32[]{:S(2)}) async-start(bf16[32,10,10,384]{3,2,1,0:T(8,128)(2,1)} %scatter_fusion), calls=%async_computation | async-start | bytes 7864320 | tf_op jit(solution)/shard_map/all_to_all | solution.py:116
  130.4 103.6 %all-gather.3.cloned.1.call-start = ((), (), s32[]{:S(2)}) async-start(), calls=%async_computation.4 | async-start | bytes 1966080 | tf_op jit(solution)/shard_map/all_gather | solution.py:123
  131.8 89.5 %copy-start.80 = (f32[384]{0:T(512)}, f32[384]{0:T(512)S(1)}, u32[]{:S(2)}) copy-start(f32[384]{0:T(512)S(1)} %get-tuple-element.654) | copy-start | bytes 4612
  131.8 89.5 %copy-start.84 = (f32[384]{0:T(512)}, f32[384]{0:T(512)S(1)}, u32[]{:S(2)}) copy-start(f32[384]{0:T(512)S(1)} %get-tuple-element.655) | copy-start | bytes 4612
  131.8 89.5 %copy-start.86 = (f32[384]{0:T(512)}, f32[384]{0:T(512)S(1)}, u32[]{:S(2)}) copy-start(f32[384]{0:T(512)S(1)} %get-tuple-element.656) | copy-start | bytes 4612
  131.9 89.4 %copy-start.44 = (f32[384]{0:T(512)}, f32[384]{0:T(512)S(1)}, u32[]{:S(2)}) copy-start(f32[384]{0:T(512)S(1)} %get-tuple-element.635) | copy-start | bytes 4612
  131.9 89.4 %copy-start.48 = (f32[384]{0:T(512)}, f32[384]{0:T(512)S(1)}, u32[]{:S(2)}) copy-start(f32[384]{0:T(512)S(1)} %get-tuple-element.636) | copy-start | bytes 4612
  131.9 89.4 %copy-start.50 = (f32[384]{0:T(512)}, f32[384]{0:T(512)S(1)}, u32[]{:S(2)}) copy-start(f32[384]{0:T(512)S(1)} %get-tuple-element.637) | copy-start | bytes 4612
  131.9 89.4 %copy-start.52 = (f32[384]{0:T(512)}, f32[384]{0:T(512)S(1)}, u32[]{:S(2)}) copy-start(f32[384]{0:T(512)S(1)} %get-tuple-element.638) | copy-start | bytes 4612
  131.9 89.4 %copy-start.54 = (f32[384]{0:T(512)}, f32[384]{0:T(512)S(1)}, u32[]{:S(2)}) copy-start(f32[384]{0:T(512)S(1)} %get-tuple-element.639) | copy-start | bytes 4612
  132.0 89.4 %copy-start.56 = (f32[384]{0:T(512)}, f32[384]{0:T(512)S(1)}, u32[]{:S(2)}) copy-start(f32[384]{0:T(512)S(1)} %get-tuple-element.640) | copy-start | bytes 4612
  132.0 89.4 %copy-start.58 = (f32[384]{0:T(512)}, f32[384]{0:T(512)S(1)}, u32[]{:S(2)}) copy-start(f32[384]{0:T(512)S(1)} %get-tuple-element.641) | copy-start | bytes 4612
  132.0 89.4 %copy-start.60 = (f32[384]{0:T(512)}, f32[384]{0:T(512)S(1)}, u32[]{:S(2)}) copy-start(f32[384]{0:T(512)S(1)} %get-tuple-element.642) | copy-start | bytes 4612
  132.0 89.4 %copy-start.62 = (f32[384]{0:T(512)}, f32[384]{0:T(512)S(1)}, u32[]{:S(2)}) copy-start(f32[384]{0:T(512)S(1)} %get-tuple-element.643) | copy-start | bytes 4612
  132.0 89.4 %copy-start.64 = (f32[384]{0:T(512)}, f32[384]{0:T(512)S(1)}, u32[]{:S(2)}) copy-start(f32[384]{0:T(512)S(1)} %get-tuple-element.644) | copy-start | bytes 4612
  132.0 89.4 %copy-start.66 = (f32[384]{0:T(512)}, f32[384]{0:T(512)S(1)}, u32[]{:S(2)}) copy-start(f32[384]{0:T(512)S(1)} %get-tuple-element.645) | copy-start | bytes 4612
  132.0 89.4 %copy-start.68 = (f32[384]{0:T(512)}, f32[384]{0:T(512)S(1)}, u32[]{:S(2)}) copy-start(f32[384]{0:T(512)S(1)} %get-tuple-element.646) | copy-start | bytes 4612
  134.5 217.5 %all-reduce.4.cloned.1.call-start = ((), (), s32[]{:S(2)}) async-start(), calls=%async_computation.3 | async-start | bytes 6291456 | tf_op jit(solution)/shard_map/psum | solution.py:146
  216.7 17.2 %collective-permute-start = (bf16[32,4,4,384]{3,2,1,0:T(4,128)(2,1)S(1)}, bf16[32,4,4,384]{3,2,1,0:T(4,128)(2,1)S(1)}, u32[]{:S(2)}, u32[]{:S(2)}) collective-permute-start(bf16[32,4,4,384]{3,2,1,0:T(4,128)(2,1)S(1)} %add_convert_fusion.2), channel_id=1, source_target_pairs={{0,1},{1,2},{2,3},{3,0},{4,5},{5,6},{6,7},{7,4},{8,9},{9,10},{10,1... | collective-permute-start | bytes 1179656 | tf_op jit(solution)/shard_map/ppermute | solution.py:25
  218.7 19.0 %collective-permute-start.2 = (bf16[32,4,4,384]{3,2,1,0:T(4,128)(2,1)S(1)}, bf16[32,4,4,384]{3,2,1,0:T(4,128)(2,1)S(1)}, u32[]{:S(2)}, u32[]{:S(2)}) collective-permute-start(bf16[32,4,4,384]{3,2,1,0:T(4,128)(2,1)S(1)} %add_convert_fusion.2), channel_id=1, source_target_pairs={{1,0},{2,1},{3,2},{0,3},{5,4},{6,5},{7,6},{4,7},{9,8},{10,9},{11,1... | collective-permute-start | bytes 1179656 | tf_op jit(solution)/shard_map/ppermute | solution.py:27
  233.9 9.2 collective-permute-start.1
  849.4 106.5 %all-to-all-start.2 = ((f32[32,10,10,384]{3,2,1,0:T(8,128)}), f32[32,10,10,384]{3,2,1,0:T(8,128)}, u32[]{:S(2)}, u32[]{:S(2)}) async-start(f32[32,10,10,384]{3,2,1,0:T(8,128)} %scatter_fusion.2), calls=%async_computation.2 | async-start | bytes 15728640 | tf_op jit(solution)/shard_map/all_to_all | solution.py:162
  (85 other events, 3403.2 us)
Sparse Core Ops, SparseCore 0:
  134.6 32.7 all-gather.2
  279.0 73.0 all-reduce.3
